TPU v7x, 256 devices: a whole 4x4x8 slice. The times are simulated.
256 devices in a mesh: dp: 8 (over y, core), tower: 2 (over x_lo), seq: 16 (over x_hi, z).
Axes of the slice: x: 4 (x_hi: 2, x_lo: 2; x = x_hi * 2 + x_lo), y: 4, z: 8, core: 2. Of those that a mesh axis runs over, the one named last changes fastest.
Arguments:
- query_proj: bfloat16 [8, 2, 2048, 1536], P('dp', 'tower', 'seq'), may hold values from -90 to 90
- key_proj: bfloat16 [8, 2, 2048, 1536], P('dp', 'tower', 'seq'), may hold values from -9 to 9
- value_proj: bfloat16 [8, 2, 2048, 1536], P('dp', 'tower', 'seq'), may hold values from -6 to 6
- out_grad: bfloat16 [8, 2, 2048, 1536], P('dp', 'tower', 'seq'), may hold values from -6 to 6
- gate_scale: float32 [2, 1536], P('tower'), may hold values from 2 to 16
Outputs:
- attended: bfloat16 [8, 2, 2048, 1536], P('dp', 'tower', 'seq')
- query_grad: bfloat16 [8, 2, 2048, 1536], P('dp', 'tower', 'seq')
- key_grad: bfloat16 [8, 2, 2048, 1536], P('dp', 'tower', 'seq')
- value_grad: bfloat16 [8, 2, 2048, 1536], P('dp', 'tower', 'seq')
- gate_grad: float32 [2, 1536], P('tower')
All inputs are finite; a program needn't handle non-finite values.
Results may differ from a plain program's by a relative error of at most 0.035.
Values may be sent and summed in bfloat16 or wider, within the bound.
A program may use at most 128 MiB of HBM per device.

v0:
```python
import math

import jax
import jax.numpy as jnp
from jax import lax
from jax.sharding import PartitionSpec as P

HEAD_DIM = 128


def from_partner(block, axis, bit):
    count = lax.axis_size(axis)
    route = []
    for low in range(count):
        high = low | 1 << bit
        if high != low and high < count:
            route += [(low, high), (high, low)]
    return lax.ppermute(block, axis, route)


def local(query_proj, key_proj, value_proj, out_grad, gate_scale):
    queries_local = query_proj[0, 0]
    cotangent_local = out_grad[0, 0]
    gate_local = gate_scale[0]
    row_count, feature_count = queries_local.shape
    head_count = feature_count // HEAD_DIM
    group_size = 4
    group_total = head_count // group_size
    span = group_size * HEAD_DIM
    score_scale = 1.0 / math.sqrt(HEAD_DIM)
    own_pair = jnp.stack([key_proj[0, 0], value_proj[0, 0]])
    partner = from_partner(own_pair, "tower", 0)
    total_keys = row_count * lax.axis_size("seq")
    gathered = lax.all_gather(partner, "seq", axis=1, tiled=True)

    def one_group(group_index, running):
        attended_acc, query_acc, pair_acc, gate_acc = running
        offset = group_index * span
        query_group = lax.dynamic_slice_in_dim(queries_local, offset, span, 1).reshape(
            row_count, group_size, HEAD_DIM
        )
        pair_group = lax.dynamic_slice_in_dim(gathered, offset, span, 2).reshape(
            2, total_keys, group_size, HEAD_DIM
        )
        cotangent_group = lax.dynamic_slice_in_dim(cotangent_local, offset, span, 1).astype(
            jnp.float32
        )
        gate_group = lax.dynamic_slice_in_dim(gate_local, offset, span, 0)
        scores = (
            jnp.einsum(
                "ihd,jhd->hij", query_group, pair_group[0], preferred_element_type=jnp.float32
            )
            * score_scale
        )
        weights = jnp.exp(scores - jnp.max(scores, axis=-1, keepdims=True))
        group_mass = jnp.sum(weights, axis=-1)
        probs = weights / group_mass[:, :, None]
        probs_low = probs.astype(jnp.bfloat16)
        mixed = jnp.einsum(
            "hij,jhd->ihd", probs_low, pair_group[1], preferred_element_type=jnp.float32
        ).reshape(row_count, span)
        attended_group = (gate_group * mixed).astype(jnp.bfloat16)
        grad_heads = (gate_group * cotangent_group).astype(jnp.bfloat16)
        gate_term = jnp.sum(cotangent_group * mixed, axis=0)
        grad_shaped = grad_heads.reshape(row_count, group_size, HEAD_DIM)
        delta = jnp.sum(
            grad_heads.astype(jnp.float32).reshape(row_count, group_size, HEAD_DIM)
            * mixed.reshape(row_count, group_size, HEAD_DIM),
            axis=-1,
        ).T
        grad_probs = jnp.einsum(
            "ihd,jhd->hij", grad_shaped, pair_group[1], preferred_element_type=jnp.float32
        )
        grad_scores = (probs * (grad_probs - delta[:, :, None]) * score_scale).astype(jnp.bfloat16)
        query_part = (
            jnp.einsum(
                "hij,jhd->ihd", grad_scores, pair_group[0], preferred_element_type=jnp.float32
            )
            .reshape(row_count, span)
            .astype(jnp.bfloat16)
        )
        key_part = jnp.einsum(
            "hij,ihd->jhd", grad_scores, query_group, preferred_element_type=jnp.float32
        )
        value_part = jnp.einsum(
            "hij,ihd->jhd", probs_low, grad_shaped, preferred_element_type=jnp.float32
        )
        pair_part = (
            jnp.stack([key_part, value_part]).reshape(2, total_keys, span).astype(jnp.bfloat16)
        )
        pair_acc = lax.dynamic_update_slice_in_dim(pair_acc, pair_part, offset, 2)
        attended_acc = lax.dynamic_update_slice_in_dim(attended_acc, attended_group, offset, 1)
        query_acc = lax.dynamic_update_slice_in_dim(query_acc, query_part, offset, 1)
        gate_acc = lax.dynamic_update_slice_in_dim(gate_acc, gate_term, offset, 0)
        return (attended_acc, query_acc, pair_acc, gate_acc)

    pair_start = jnp.zeros((2, total_keys, feature_count), jnp.bfloat16)
    initial = (
        jnp.zeros((row_count, feature_count), jnp.bfloat16),
        jnp.zeros((row_count, feature_count), jnp.bfloat16),
        pair_start,
        jnp.zeros((feature_count,), jnp.float32),
    )
    attended_rows, query_rows, pair_terms, gate_terms = lax.fori_loop(
        0, group_total, one_group, initial
    )
    pair_sums = lax.psum_scatter(pair_terms, "seq", scatter_dimension=1, tiled=True).astype(
        jnp.float32
    )
    returned = from_partner(pair_sums.astype(jnp.bfloat16), "tower", 0)
    gate_total = lax.psum(gate_terms, ("dp", "seq"))
    return (
        attended_rows[None, None],
        query_rows[None, None],
        returned[0][None, None],
        returned[1][None, None],
        gate_total[None],
    )


def solution(mesh):
    return jax.shard_map(
        local,
        mesh=mesh,
        in_specs=(
            P("dp", "tower", "seq", None),
            P("dp", "tower", "seq", None),
            P("dp", "tower", "seq", None),
            P("dp", "tower", "seq", None),
            P("tower", None),
        ),
        out_specs=(
            P("dp", "tower", "seq", None),
            P("dp", "tower", "seq", None),
            P("dp", "tower", "seq", None),
            P("dp", "tower", "seq", None),
            P("tower", None),
        ),
        check_vma=False,
    )
```

profile of v0, /device:TPU:2, one launch (start us, length us, event | category | flops | bytes accessed | tf_op | source)
XLA Modules:
  0.0 911.0 jit_solution(759841324773712574)
XLA Ops:
  9.9 2.4 collective-permute-start
  12.2 17.0 %collective-permute-done = bf16[2,128,1536]{1,2,0:T(8,128)(2,1)S(1)} collective-permute-done((bf16[2,128,1536]{1,2,0:T(8,128)(2,1)S(1)}, bf16[2,128,1536]{1,2,0:T(8,128)(2,1)S(1)}, u32[]{:S(2)}, u32[]{:S(2)}) %collective-permute-start) | collective-permute-done | bytes 786464 | tf_op jit(solution)/shard_map/ppermute | solution.py:18
  30.7 194.9 %all-gather.2.cloned.1.call-done = bf16[2,2048,1536]{1,2,0:T(8,128)(2,1)} async-done(((bf16[2,128,1536]{1,2,0:T(8,128)(2,1)}), bf16[2,2048,1536]{1,2,0:T(8,128)(2,1)}) %all-gather.2.cloned.1.call-update) | async-done | bytes 12582928 | tf_op jit(solution)/shard_map/all_gather | solution.py:34
  227.2 5.3 broadcast_in_dim.28.clone
  232.5 91.6 %while.19 = (s32[]{:T(128)}, bf16[128,1536]{1,0:T(8,128)(2,1)}, bf16[128,1536]{1,0:T(8,128)(2,1)}, bf16[2,2048,1536]{2,1,0:T(8,128)(2,1)}, f32[1536]{0:T(1024)S(...) while((s32[]{:T(128)}, bf16[128,1536]{1,0:T(8,128)(2,1)}, ...), condition=%wide.region_5.0_spmd, body=%wide.region_0.0_spmd.sunk | while | flops 1626080256 | bytes 99508504 | solution.py:104
  232.6 4.0 constant_dynamic-slice_fusion.5
  236.6 3.5 fusion.53
  240.1 2.9 fusion.54
  248.5 2.3 pad_maximum_fusion.3
  250.8 6.3 copy.46
  258.5 4.6 constant_dynamic-update-slice_fusion.6
  263.2 4.0 constant_dynamic-slice_fusion.5
  267.2 3.5 fusion.53
  270.7 2.9 fusion.54
  279.0 2.3 pad_maximum_fusion.3
  281.3 6.3 copy.46
  289.1 4.5 constant_dynamic-update-slice_fusion.6
  293.7 4.0 constant_dynamic-slice_fusion.5
  297.8 3.5 fusion.53
  301.2 2.9 fusion.54
  311.9 6.3 copy.46
  319.6 4.5 constant_dynamic-update-slice_fusion.6
  324.2 248.2 %reduce-scatter.2.cloned.1.call-done = bf16[2,128,1536]{2,1,0:T(8,128)(2,1)} async-done(((bf16[2,2048,1536]{2,1,0:T(8,128)(2,1)}), bf16[2,128,1536]{2,1,0:T(8,128)(2,1)}) %reduce-scatter.2.cloned.1.call-update) | async-done | bytes 786448 | tf_op jit(solution)/shard_map/reduce_scatter | solution.py:107
  573.8 329.3 %psum.7 = f32[1,1536]{1,0:T(1,128)} all-reduce(f32[1,1536]{1,0:T(1,128)S(1)} %broadcast_in_dim.32), channel_id=1, replica_groups=mesh['dp'=8,'tower'=2,'seq'=16] {'dp','seq'}, use_global_device_ids=true, to_apply=%region_7.0 | all-reduce | flops 1536 | bytes 12288 | tf_op jit(solution)/shard_map/psum | solution.py:111
  (74 shorter events, 31.1 us)
Async XLA Ops:
  7.2 23.1 %copy-start.3 = (bf16[1,1,128,1536]{3,2,1,0:T(8,128)(2,1)S(1)}, bf16[1,1,128,1536]{3,2,1,0:T(8,128)(2,1)}, u32[]{:S(2)}) copy-start(bf16[1,1,128,1536]{3,2,1,0:T(8,128)(2,1)} %param.7) | copy-start | bytes 1179652
  7.2 218.5 %all-gather.2.cloned.1.call-start = ((), (), s32[]{:S(2)}) async-start(), calls=%async_computation.1 | async-start | bytes 13369344 | tf_op jit(solution)/shard_map/all_gather | solution.py:34
  8.5 22.0 %copy-start.4 = (bf16[1,1,128,1536]{3,2,1,0:T(8,128)(2,1)S(1)}, bf16[1,1,128,1536]{3,2,1,0:T(8,128)(2,1)}, u32[]{:S(2)}) copy-start(bf16[1,1,128,1536]{3,2,1,0:T(8,128)(2,1)} %param.10) | copy-start | bytes 1179652
  9.8 20.9 %copy-start.5 = (f32[1,1536]{1,0:T(1,128)S(1)}, f32[1,1536]{1,0:T(1,128)}, u32[]{:S(2)}) copy-start(f32[1,1536]{1,0:T(1,128)} %param.11) | copy-start | bytes 18436
  9.9 19.4 %collective-permute-start = (bf16[2,128,1536]{1,2,0:T(8,128)(2,1)S(1)}, bf16[2,128,1536]{1,2,0:T(8,128)(2,1)S(1)}, u32[]{:S(2)}, u32[]{:S(2)}) collective-permute-start(bf16[2,128,1536]{1,2,0:T(8,128)(2,1)S(1)} %pad_maximum_fusion.1), channel_id=1, source_target_pairs={{0,16},{16,0},{1,17},{17,1},{2,18},{18,2},{3,19},{19,3},{4,20},{20... | collective-permute-start | bytes 2359304 | tf_op jit(solution)/shard_map/ppermute | solution.py:18
  29.2 0.9 copy-start.2
  30.2 542.2 %reduce-scatter.2.cloned.1.call-start = ((), (), s32[]{:S(2)}) async-start(), calls=%async_computation.2 | async-start | bytes 13369344 | tf_op jit(solution)/shard_map/reduce_scatter | solution.py:107
  240.1 2.9 copy-start.1
  243.8 2.2 copy-start
  270.7 2.9 copy-start.1
  274.4 2.2 copy-start
  301.2 2.9 copy-start.1
  304.9 2.2 copy-start
  572.4 330.8 %collective-permute-start.1 = (bf16[2,128,1536]{2,1,0:T(8,128)(2,1)}, bf16[2,128,1536]{2,1,0:T(8,128)(2,1)S(1)}, u32[]{:S(2)}, u32[]{:S(2)}) collective-permute-start(bf16[2,128,1536]{2,1,0:T(8,128)(2,1)} %reduce-scatter.2.cloned.1.call-done), channel_id=1, source_target_pairs={{0,16},{16,0},{1,17},{17,1},{2,18},{18,2},{3,19},{19,3},{4,20},{20... | collective-permute-start | bytes 2359304 | tf_op jit(solution)/shard_map/ppermute | solution.py:18
Sparse Core Ops, SparseCore 0:
  30.3 195.3 all-gather.1
  324.3 248.0 reduce-scatter.1
where the time goes:
time: 912 us; the launch traced here: 911 us
  waiting for transfers between devices  460 us (50%)
  blocking collectives  329 us (36%)
  local copies, waits for them, and re-layouts  64.5 us (7%)
  matrix products  22.1 us (2%)
  other arithmetic  16.5 us (2%)
  between operations  14.1 us (2%)
    psum x1, blocking collectives, local(): gate_total = lax.psum(gate_terms, ('dp', 'seq'))  329 us
    reduce_scatter x1, waiting for transfers between devices, local(): lax.psum_scatter(pair_terms, 'seq', scatter_dimension=1, tiled=True)  248 us
    all_gather x1, waiting for transfers between devices, local(): gathered = lax.all_gather(partner, 'seq', axis=1, tiled=True)  195 us
    dynamic_update_slice x6, local copies, waits for them, and re-layouts, one_group(): pair_acc = lax.dynamic_update_slice_in_dim(pair_acc, pair_part, offset, 2)  32.5 us
  transfers between devices with their start and end apart: 4, of which 3 were waited for; matrix products, arithmetic and copies ran while one was open for 0% of the time, Pallas kernels for 0%

commit v1 on v0

v1 whole, which is shorter than its diff:
```python
import math

import jax
import jax.numpy as jnp
from jax import lax
from jax.experimental import pallas as pl
from jax.experimental.pallas import tpu as pltpu
from jax.sharding import PartitionSpec as P

HEADS = 12
HEAD_DIM = 128
ROWS = 128
BLOCKS = 16
TOKENS = ROWS * BLOCKS
D = HEADS * HEAD_DIM
Z = 8
CLIPS = 8
CHUNK = 256
CHUNKS = TOKENS // CHUNK
PER_CHUNK = CHUNK // ROWS
SCALE = 1.0 / math.sqrt(HEAD_DIM)
EXP2_SCALE = SCALE * math.log2(math.e)
MESH = pl.DeviceIdType.MESH


def place_of(tower, x_hi, slot, core):
    ring = (slot // 3) * 4 + slot % 3 + 1
    z = (ring + 2 * x_hi + tower + 16 - 2 * core) % Z
    return x_hi * Z + z


def rows_of(block):
    return pl.ds(pl.multiple_of(block * ROWS, ROWS), ROWS)


def lanes_of(head):
    return pl.ds(pl.multiple_of(head * HEAD_DIM, HEAD_DIM), HEAD_DIM)


def kernel(
    query_ref,
    key_ref,
    value_ref,
    cot_ref,
    gate_ref,
    att_ref,
    dq_ref,
    dk_ref,
    dv_ref,
    gate_grad_ref,
    q_all,
    k_all,
    v_all,
    g_all,
    att_all,
    dq_all,
    dk_acc,
    dv_acc,
    dk_all,
    dv_all,
    gate_acc,
    gate_in,
    gate_total,
    gate_heads,
    kv_send,
    qg_send,
    k_recv,
    v_recv,
    q_recv,
    g_recv,
    rows_send,
    cols_send,
    out_recv,
    clip_send,
    clip_recv,
    head_send,
    head_recv,
):
    clip = lax.axis_index("dp")
    tower = lax.axis_index("tower")
    seq = lax.axis_index("seq")
    core = clip % 2
    x_hi = seq // Z
    z = seq % Z
    ring = (z + 2 * core + 16 - 2 * x_hi - tower) % Z
    has_unit = ring % 4 != 0
    slot = (ring // 4) * 3 + lax.max(ring % 4 - 1, 0)
    head = x_hi * 6 + slot

    def device(clip_to, tower_to, seq_to):
        return {"dp": clip_to, "tower": tower_to, "seq": seq_to}

    def peer_clip(step):
        other = (clip + step) % CLIPS
        other_z = (z + 2 * core + 16 - 2 * (other % 2)) % Z
        return other, x_hi * Z + other_z

    barrier = pltpu.get_barrier_semaphore()

    def greet(step, carry):
        place = (tower * BLOCKS + seq + step) % (2 * BLOCKS)
        pl.semaphore_signal(
            barrier,
            inc=1,
            device_id=device(clip, place // BLOCKS, place % BLOCKS),
            device_id_type=MESH,
        )
        return carry

    lax.fori_loop(1, 2 * BLOCKS, greet, 0)

    def greet_clip(step, carry):
        other, place = peer_clip(step)
        pl.semaphore_signal(
            barrier, inc=1, device_id=device(other, tower, place), device_id_type=MESH
        )
        return carry

    lax.fori_loop(1, CLIPS, greet_clip, 0)
    pl.semaphore_wait(barrier, 2 * BLOCKS - 1 + CLIPS - 1)

    def target(step, tower_to):
        half = step // 2
        to_x = (x_hi + step) % 2
        turn = (half // 2) * (1 - 2 * (half % 2)) + 5 * (half % 2)
        to_ring = (z + 2 * core + 16 - 2 * to_x - tower_to) % Z
        to_slot = ((to_ring * 3) // 4 + turn) % 6
        return to_x * 6 + to_slot, place_of(tower_to, to_x, to_slot, core)

    def send_kv(step, carry):
        to_head, place = target(step, 1 - tower)
        for index, (source, sink, arrived) in enumerate(
            ((key_ref, k_all, k_recv), (value_ref, v_all, v_recv))
        ):
            pltpu.make_async_remote_copy(
                src_ref=source.at[0, 0, :, lanes_of(to_head)],
                dst_ref=sink.at[rows_of(seq)],
                send_sem=kv_send.at[index, to_head],
                recv_sem=arrived.at[seq],
                device_id=device(clip, 1 - tower, place),
                device_id_type=MESH,
            ).start()
        return carry

    lax.fori_loop(0, HEADS, send_kv, 0)

    def query_copy(index, to_head, place):
        source, sink, arrived = ((query_ref, q_all, q_recv), (cot_ref, g_all, g_recv))[index]
        return pltpu.make_async_remote_copy(
            src_ref=source.at[0, 0, :, lanes_of(to_head)],
            dst_ref=sink.at[rows_of(seq)],
            send_sem=qg_send.at[index, to_head],
            recv_sem=arrived.at[seq],
            device_id=device(clip, tower, place),
            device_id_type=MESH,
        )

    def send_qg(step, carry):
        to_head, place = target(step, tower)

        @pl.when(place != seq)
        def _():
            for index in range(2):
                query_copy(index, to_head, place).start()

        @pl.when(place == seq)
        def _():
            for source, sink, arrived in ((query_ref, q_all, q_recv), (cot_ref, g_all, g_recv)):
                pltpu.make_async_copy(
                    source.at[0, 0, :, lanes_of(to_head)],
                    sink.at[rows_of(seq)],
                    arrived.at[seq],
                ).start()

        return carry

    lax.fori_loop(0, HEADS, send_qg, 0)

    def row_copy(index, block):
        source, sink = ((att_all, att_ref), (dq_all, dq_ref))[index]
        return pltpu.make_async_remote_copy(
            src_ref=source.at[rows_of(block)],
            dst_ref=sink.at[0, 0, :, lanes_of(head)],
            send_sem=rows_send.at[index, block],
            recv_sem=out_recv.at[index, head],
            device_id=device(clip, tower, block),
            device_id_type=MESH,
        )

    def column_copy(index, block):
        source, sink = ((dk_all, dk_ref), (dv_all, dv_ref))[index]
        return pltpu.make_async_remote_copy(
            src_ref=source.at[rows_of(block)],
            dst_ref=sink.at[0, 0, :, lanes_of(head)],
            send_sem=cols_send.at[index, block],
            recv_sem=out_recv.at[2 + index, head],
            device_id=device(clip, 1 - tower, block),
            device_id_type=MESH,
        )

    def clip_copy(step):
        other, place = peer_clip(step)
        return pltpu.make_async_remote_copy(
            src_ref=gate_acc,
            dst_ref=gate_in.at[clip],
            send_sem=clip_send.at[step],
            recv_sem=clip_recv.at[clip],
            device_id=device(other, tower, place),
            device_id_type=MESH,
        )

    def head_copy(step):
        place = (seq + step) % BLOCKS
        return pltpu.make_async_remote_copy(
            src_ref=gate_total,
            dst_ref=gate_heads.at[head],
            send_sem=head_send.at[step],
            recv_sem=head_recv.at[head],
            device_id=device(clip, tower, place),
            device_id_type=MESH,
        )

    @pl.when(has_unit)
    def _():
        gate_row = gate_ref[:, lanes_of(head)]
        gate_acc[...] = jnp.zeros_like(gate_acc)
        dk_acc[...] = jnp.zeros_like(dk_acc)
        dv_acc[...] = jnp.zeros_like(dv_acc)

        def wait_kv(block, carry):
            pltpu.make_async_copy(
                k_all.at[rows_of(block)], k_all.at[rows_of(block)], k_recv.at[block]
            ).wait()
            pltpu.make_async_copy(
                v_all.at[rows_of(block)], v_all.at[rows_of(block)], v_recv.at[block]
            ).wait()
            return carry

        lax.fori_loop(0, BLOCKS, wait_kv, 0)

        def one_chunk(step, carry):
            chunk = (seq // PER_CHUNK + step) % CHUNKS
            for part in range(PER_CHUNK):
                block = chunk * PER_CHUNK + part
                pltpu.make_async_copy(
                    q_all.at[rows_of(block)], q_all.at[rows_of(block)], q_recv.at[block]
                ).wait()
                pltpu.make_async_copy(
                    g_all.at[rows_of(block)], g_all.at[rows_of(block)], g_recv.at[block]
                ).wait()
            rows = pl.ds(pl.multiple_of(chunk * CHUNK, CHUNK), CHUNK)
            queries = q_all[rows, :]
            keys = k_all[...]
            values = v_all[...]
            cot = g_all[rows, :].astype(jnp.float32)
            grad_heads = (gate_row * cot).astype(jnp.bfloat16)
            scores = lax.dot_general(
                queries, keys, (((1,), (1,)), ((), ())), preferred_element_type=jnp.float32
            )
            row_top = jnp.max(scores, axis=-1, keepdims=True)
            weights = jnp.exp2((scores - row_top) * EXP2_SCALE)
            mass = jnp.sum(weights, axis=-1, keepdims=True)
            probs = weights * (1.0 / mass)
            probs_low = probs.astype(jnp.bfloat16)
            mixed = jnp.dot(probs_low, values, preferred_element_type=jnp.float32)
            att_all[rows, :] = (gate_row * mixed).astype(jnp.bfloat16)
            gate_acc[...] += jnp.sum((cot * mixed).reshape(CHUNK // 8, 8, HEAD_DIM), axis=0)
            delta = jnp.sum(grad_heads.astype(jnp.float32) * mixed, axis=-1, keepdims=True)
            grad_probs = lax.dot_general(
                grad_heads, values, (((1,), (1,)), ((), ())), preferred_element_type=jnp.float32
            )
            grad_scores = (probs * (grad_probs - delta) * SCALE).astype(jnp.bfloat16)
            dq_all[rows, :] = jnp.dot(
                grad_scores, keys, preferred_element_type=jnp.float32
            ).astype(jnp.bfloat16)
            for part in range(PER_CHUNK):
                block = chunk * PER_CHUNK + part

                @pl.when(block != seq)
                def _():
                    for index in range(2):
                        row_copy(index, block).start()

                @pl.when(block == seq)
                def _():
                    for index, (source, sink) in enumerate(((att_all, att_ref), (dq_all, dq_ref))):
                        pltpu.make_async_copy(
                            source.at[rows_of(block)],
                            sink.at[0, 0, :, lanes_of(head)],
                            out_recv.at[index, head],
                        ).start()

            dk_acc[...] += lax.dot_general(
                grad_scores, queries, (((0,), (0,)), ((), ())), preferred_element_type=jnp.float32
            )
            dv_acc[...] += lax.dot_general(
                probs_low, grad_heads, (((0,), (0,)), ((), ())), preferred_element_type=jnp.float32
            )
            return carry

        lax.fori_loop(0, CHUNKS, one_chunk, 0)

        gate_in[pl.ds(clip, 1)] = gate_acc[...][None]

        def send_clip(step, carry):
            clip_copy(step).start()
            return carry

        lax.fori_loop(1, CLIPS, send_clip, 0)

        dk_all[...] = dk_acc[...].astype(jnp.bfloat16)
        dv_all[...] = dv_acc[...].astype(jnp.bfloat16)

        def send_columns(step, carry):
            block = (seq + step) % BLOCKS
            column_copy(0, block).start()
            column_copy(1, block).start()
            return carry

        lax.fori_loop(0, BLOCKS, send_columns, 0)

        def wait_clip(step, carry):
            other = (clip + step) % CLIPS
            pltpu.make_async_copy(gate_in.at[other], gate_in.at[other], clip_recv.at[other]).wait()
            return carry

        lax.fori_loop(1, CLIPS, wait_clip, 0)
        total = jnp.sum(jnp.sum(gate_in[...], axis=0), axis=0, keepdims=True)
        total = jnp.broadcast_to(total, (8, HEAD_DIM))
        gate_total[...] = total
        gate_heads[pl.ds(head, 1)] = total[None]

        def send_head(step, carry):
            head_copy(step).start()
            return carry

        lax.fori_loop(1, BLOCKS, send_head, 0)

    def wait_outputs(from_head, carry):
        for index, sink in enumerate((att_ref, dq_ref, dk_ref, dv_ref)):
            there = sink.at[0, 0, :, lanes_of(from_head)]
            pltpu.make_async_copy(there, there, out_recv.at[index, from_head]).wait()

        @pl.when(jnp.logical_or(from_head != head, jnp.logical_not(has_unit)))
        def _():
            there = gate_heads.at[from_head]
            pltpu.make_async_copy(there, there, head_recv.at[from_head]).wait()

        return carry

    lax.fori_loop(0, HEADS, wait_outputs, 0)
    for from_head in range(HEADS):
        gate_grad_ref[:, from_head * HEAD_DIM : (from_head + 1) * HEAD_DIM] = gate_heads[
            from_head, 0:1
        ]

    def wait_inputs_sent(step, carry):
        to_head, place = target(step, 1 - tower)
        for index, source in enumerate((key_ref, value_ref)):
            part = source.at[0, 0, :, lanes_of(to_head)]
            pltpu.make_async_copy(part, part, kv_send.at[index, to_head]).wait()
        to_head, place = target(step, tower)

        @pl.when(place != seq)
        def _():
            for index in range(2):
                query_copy(index, to_head, place).wait_send()

        return carry

    lax.fori_loop(0, HEADS, wait_inputs_sent, 0)

    @pl.when(has_unit)
    def _():
        def wait_sent(block, carry):
            for index in range(2):

                @pl.when(block != seq)
                def _():
                    row_copy(index, block).wait_send()

                column_copy(index, block).wait_send()
            return carry

        lax.fori_loop(0, BLOCKS, wait_sent, 0)

        def wait_clip_sent(step, carry):
            clip_copy(step).wait_send()
            return carry

        lax.fori_loop(1, CLIPS, wait_clip_sent, 0)

        def wait_head_sent(step, carry):
            head_copy(step).wait_send()
            return carry

        lax.fori_loop(1, BLOCKS, wait_head_sent, 0)


def local(query_proj, key_proj, value_proj, out_grad, gate_scale):
    whole = pl.BlockSpec(memory_space=pl.ANY)
    small = pl.BlockSpec(memory_space=pltpu.VMEM)
    big = jax.ShapeDtypeStruct((1, 1, ROWS, D), jnp.bfloat16)
    unit_rows = pltpu.VMEM((TOKENS, HEAD_DIM), jnp.bfloat16)
    unit_sums = pltpu.VMEM((TOKENS, HEAD_DIM), jnp.float32)
    gate_tile = pltpu.VMEM((8, HEAD_DIM), jnp.float32)
    dma = pltpu.SemaphoreType.DMA
    return pl.pallas_call(
        kernel,
        out_shape=(big, big, big, big, jax.ShapeDtypeStruct((1, D), jnp.float32)),
        in_specs=[whole] * 4 + [small],
        out_specs=(whole, whole, whole, whole, small),
        scratch_shapes=[
            unit_rows,
            unit_rows,
            unit_rows,
            unit_rows,
            unit_rows,
            unit_rows,
            unit_sums,
            unit_sums,
            unit_rows,
            unit_rows,
            gate_tile,
            pltpu.VMEM((CLIPS, 8, HEAD_DIM), jnp.float32),
            gate_tile,
            pltpu.VMEM((HEADS, 8, HEAD_DIM), jnp.float32),
            dma((2, HEADS)),
            dma((2, HEADS)),
            dma((BLOCKS,)),
            dma((BLOCKS,)),
            dma((BLOCKS,)),
            dma((BLOCKS,)),
            dma((2, BLOCKS)),
            dma((2, BLOCKS)),
            dma((4, HEADS)),
            dma((CLIPS,)),
            dma((CLIPS,)),
            dma((BLOCKS,)),
            dma((HEADS,)),
        ],
        compiler_params=pltpu.CompilerParams(
            collective_id=0, has_side_effects=True, vmem_limit_bytes=50 * 2**20
        ),
        cost_estimate=pl.CostEstimate(
            flops=12 * TOKENS * TOKENS * HEAD_DIM,
            bytes_accessed=16 * TOKENS * HEAD_DIM,
            transcendentals=TOKENS * TOKENS,
        ),
        name="heads_attention",
    )(query_proj, key_proj, value_proj, out_grad, gate_scale)


def solution(mesh):
    tokens = P("dp", "tower", "seq", None)
    gate = P("tower", None)
    return jax.shard_map(
        local,
        mesh=mesh,
        in_specs=(tokens, tokens, tokens, tokens, gate),
        out_specs=(tokens, tokens, tokens, tokens, gate),
        check_vma=False,
    )
```

time: 912 us -> 104 us (0.11)
  the two profiles are of different devices: /device:TPU:2 before, /device:TPU:48 now
where the time goes in v1:
time: 104 us
  Pallas kernels  95.3 us (92%)
  local copies, waits for them, and re-layouts  8.24 us (8%)
    pallas_call x1, Pallas kernels, local(): pl.pallas_call(kernel, out_shape=(big, big, big, big, jax.ShapeDtypeStruc...  95.3 us
    unnamed x15, local copies, waits for them, and re-layouts  8.24 us

profile of v1, /device:TPU:48, one launch (start us, length us, event | category | flops | bytes accessed | tf_op | source)
XLA Modules:
  0.0 104.2 jit_solution(1777225872432277537)
XLA Ops:
  0.6 0.0 copy-start
  0.6 1.0 copy-done
  1.6 0.0 copy-start.1
  1.6 1.0 copy-done.1
  2.6 0.0 copy-start.2
  2.6 1.0 copy-done.2
  3.6 0.0 copy-start.3
  3.6 1.0 copy-done.3
  4.6 0.0 copy-start.4
  4.6 0.7 copy-done.4
  5.3 95.3 %heads_attention.1 = (bf16[1,1,128,1536]{3,2,1,0:T(8,128)(2,1)S(1)}, bf16[1,1,128,1536]{3,2,1,0:T(8,128)(2,1)S(1)}, bf16[1,1,128,1536]{3,2,1,0:T(8,128)(2,1)S(1)...) custom-call(bf16[1,1,128,1536]{3,2,1,0:T(8,128)(2,1)S(1)} %copy-done, bf16[1,1,128,1536]{3,2,1,0:T(8,128)(2,1)S(1)} %copy-done.1, ...), custom_call_target="tpu_custom_call" | custom-call | flops 6442450944 | bytes 4194304 | tf_op jit(solution)/shard_map/heads_attention/pallas_call | solution.py:408
  100.6 0.7 copy.15
  101.4 0.7 copy.16
  102.1 0.7 copy.17
  102.8 0.7 copy.18
  103.6 0.6 copy.19
Async XLA Ops:
  0.6 1.0 copy-start
  1.6 1.0 copy-start.1
  2.6 1.0 copy-start.2
  3.6 1.0 copy-start.3
  4.6 0.7 copy-start.4

commit v2 on v1

--- a/solution.py
+++ b/solution.py
@@ -21,12 +21,6 @@
 SCALE = 1.0 / math.sqrt(HEAD_DIM)
 EXP2_SCALE = SCALE * math.log2(math.e)
 MESH = pl.DeviceIdType.MESH
-
-
-def place_of(tower, x_hi, slot, core):
-    ring = (slot // 3) * 4 + slot % 3 + 1
-    z = (ring + 2 * x_hi + tower + 16 - 2 * core) % Z
-    return x_hi * Z + z
 
 
 def rows_of(block):
@@ -119,30 +113,40 @@
     lax.fori_loop(1, CLIPS, greet_clip, 0)
     pl.semaphore_wait(barrier, 2 * BLOCKS - 1 + CLIPS - 1)
 
+    def offset(turn):
+        return ((turn + 1) // 2) * (2 * (turn % 2) - 1) * (1 - 2 * core)
+
+    def offset_out(turn):
+        turn = 7 - turn
+        return ((turn + 1) // 2) * (2 * (turn % 2) - 1) * (1 - 2 * core)
+
     def target(step, tower_to):
-        half = step // 2
         to_x = (x_hi + step) % 2
-        turn = (half // 2) * (1 - 2 * (half % 2)) + 5 * (half % 2)
-        to_ring = (z + 2 * core + 16 - 2 * to_x - tower_to) % Z
-        to_slot = ((to_ring * 3) // 4 + turn) % 6
-        return to_x * 6 + to_slot, place_of(tower_to, to_x, to_slot, core)
+        to_z = (z + offset(step // 2) + Z) % Z
+        to_ring = (to_z + 2 * core + 16 - 2 * to_x - tower_to) % Z
+        to_head = to_x * 6 + (to_ring // 4) * 3 + lax.max(to_ring % 4 - 1, 0)
+        return to_ring % 4 != 0, to_head, to_x * Z + to_z
 
     def send_kv(step, carry):
-        to_head, place = target(step, 1 - tower)
-        for index, (source, sink, arrived) in enumerate(
-            ((key_ref, k_all, k_recv), (value_ref, v_all, v_recv))
-        ):
-            pltpu.make_async_remote_copy(
-                src_ref=source.at[0, 0, :, lanes_of(to_head)],
-                dst_ref=sink.at[rows_of(seq)],
-                send_sem=kv_send.at[index, to_head],
-                recv_sem=arrived.at[seq],
-                device_id=device(clip, 1 - tower, place),
-                device_id_type=MESH,
-            ).start()
+        there, to_head, place = target(step, 1 - tower)
+
+        @pl.when(there)
+        def _():
+            for index, (source, sink, arrived) in enumerate(
+                ((key_ref, k_all, k_recv), (value_ref, v_all, v_recv))
+            ):
+                pltpu.make_async_remote_copy(
+                    src_ref=source.at[0, 0, :, lanes_of(to_head)],
+                    dst_ref=sink.at[rows_of(seq)],
+                    send_sem=kv_send.at[index, to_head],
+                    recv_sem=arrived.at[seq],
+                    device_id=device(clip, 1 - tower, place),
+                    device_id_type=MESH,
+                ).start()
+
         return carry
 
-    lax.fori_loop(0, HEADS, send_kv, 0)
+    lax.fori_loop(0, BLOCKS, send_kv, 0)
 
     def query_copy(index, to_head, place):
         source, sink, arrived = ((query_ref, q_all, q_recv), (cot_ref, g_all, g_recv))[index]
@@ -156,14 +160,14 @@
         )
 
     def send_qg(step, carry):
-        to_head, place = target(step, tower)
-
-        @pl.when(place != seq)
+        there, to_head, place = target(step, tower)
+
+        @pl.when(jnp.logical_and(there, place != seq))
         def _():
             for index in range(2):
                 query_copy(index, to_head, place).start()
 
-        @pl.when(place == seq)
+        @pl.when(jnp.logical_and(there, place == seq))
         def _():
             for source, sink, arrived in ((query_ref, q_all, q_recv), (cot_ref, g_all, g_recv)):
                 pltpu.make_async_copy(
@@ -174,7 +178,7 @@
 
         return carry
 
-    lax.fori_loop(0, HEADS, send_qg, 0)
+    lax.fori_loop(0, BLOCKS, send_qg, 0)
 
     def row_copy(index, block):
         source, sink = ((att_all, att_ref), (dq_all, dq_ref))[index]
@@ -239,20 +243,27 @@
         lax.fori_loop(0, BLOCKS, wait_kv, 0)
 
         def one_chunk(step, carry):
-            chunk = (seq // PER_CHUNK + step) % CHUNKS
-            for part in range(PER_CHUNK):
-                block = chunk * PER_CHUNK + part
+            chunk = (z - offset(step) + Z) % Z
+            blocks = [part * Z + chunk for part in range(PER_CHUNK)]
+            for block in blocks:
                 pltpu.make_async_copy(
                     q_all.at[rows_of(block)], q_all.at[rows_of(block)], q_recv.at[block]
                 ).wait()
                 pltpu.make_async_copy(
                     g_all.at[rows_of(block)], g_all.at[rows_of(block)], g_recv.at[block]
                 ).wait()
-            rows = pl.ds(pl.multiple_of(chunk * CHUNK, CHUNK), CHUNK)
-            queries = q_all[rows, :]
+
+            def both(ref):
+                return jnp.concatenate([ref[rows_of(block), :] for block in blocks], axis=0)
+
+            def put(ref, values):
+                for part, block in enumerate(blocks):
+                    ref[rows_of(block), :] = values[part * ROWS : (part + 1) * ROWS]
+
+            queries = both(q_all)
             keys = k_all[...]
             values = v_all[...]
-            cot = g_all[rows, :].astype(jnp.float32)
+            cot = both(g_all).astype(jnp.float32)
             grad_heads = (gate_row * cot).astype(jnp.bfloat16)
             scores = lax.dot_general(
                 queries, keys, (((1,), (1,)), ((), ())), preferred_element_type=jnp.float32
@@ -263,18 +274,16 @@
             probs = weights * (1.0 / mass)
             probs_low = probs.astype(jnp.bfloat16)
             mixed = jnp.dot(probs_low, values, preferred_element_type=jnp.float32)
-            att_all[rows, :] = (gate_row * mixed).astype(jnp.bfloat16)
+            put(att_all, (gate_row * mixed).astype(jnp.bfloat16))
             gate_acc[...] += jnp.sum((cot * mixed).reshape(CHUNK // 8, 8, HEAD_DIM), axis=0)
             delta = jnp.sum(grad_heads.astype(jnp.float32) * mixed, axis=-1, keepdims=True)
             grad_probs = lax.dot_general(
                 grad_heads, values, (((1,), (1,)), ((), ())), preferred_element_type=jnp.float32
             )
             grad_scores = (probs * (grad_probs - delta) * SCALE).astype(jnp.bfloat16)
-            dq_all[rows, :] = jnp.dot(
-                grad_scores, keys, preferred_element_type=jnp.float32
-            ).astype(jnp.bfloat16)
-            for part in range(PER_CHUNK):
-                block = chunk * PER_CHUNK + part
+            query_grad = jnp.dot(grad_scores, keys, preferred_element_type=jnp.float32)
+            put(dq_all, query_grad.astype(jnp.bfloat16))
+            for block in blocks:
 
                 @pl.when(block != seq)
                 def _():
@@ -311,13 +320,15 @@
         dk_all[...] = dk_acc[...].astype(jnp.bfloat16)
         dv_all[...] = dv_acc[...].astype(jnp.bfloat16)
 
-        def send_columns(step, carry):
-            block = (seq + step) % BLOCKS
-            column_copy(0, block).start()
-            column_copy(1, block).start()
-            return carry
-
-        lax.fori_loop(0, BLOCKS, send_columns, 0)
+        def send_columns(index):
+            def send_column(step, carry):
+                block = ((x_hi + step) % 2) * Z + (z + offset_out(step // 2) + Z) % Z
+                column_copy(index, block).start()
+                return carry
+
+            lax.fori_loop(0, BLOCKS, send_column, 0)
+
+        send_columns(0)
 
         def wait_clip(step, carry):
             other = (clip + step) % CLIPS
@@ -335,6 +346,7 @@
             return carry
 
         lax.fori_loop(1, BLOCKS, send_head, 0)
+        send_columns(1)
 
     def wait_outputs(from_head, carry):
         for index, sink in enumerate((att_ref, dq_ref, dk_ref, dv_ref)):
@@ -355,20 +367,24 @@
         ]
 
     def wait_inputs_sent(step, carry):
-        to_head, place = target(step, 1 - tower)
-        for index, source in enumerate((key_ref, value_ref)):
-            part = source.at[0, 0, :, lanes_of(to_head)]
-            pltpu.make_async_copy(part, part, kv_send.at[index, to_head]).wait()
-        to_head, place = target(step, tower)
-
-        @pl.when(place != seq)
+        there, to_head, place = target(step, 1 - tower)
+
+        @pl.when(there)
+        def _():
+            for index, source in enumerate((key_ref, value_ref)):
+                part = source.at[0, 0, :, lanes_of(to_head)]
+                pltpu.make_async_copy(part, part, kv_send.at[index, to_head]).wait()
+
+        there, to_head, place = target(step, tower)
+
+        @pl.when(jnp.logical_and(there, place != seq))
         def _():
             for index in range(2):
                 query_copy(index, to_head, place).wait_send()
 
         return carry
 
-    lax.fori_loop(0, HEADS, wait_inputs_sent, 0)
+    lax.fori_loop(0, BLOCKS, wait_inputs_sent, 0)
 
     @pl.when(has_unit)
     def _():
@@ -397,19 +413,39 @@
         lax.fori_loop(1, BLOCKS, wait_head_sent, 0)
 
 
+def hand_on(*refs):
+    sources, sinks, held, arrived, left = refs[:5], refs[5:10], refs[10:15], refs[15], refs[16]
+    first = [
+        pltpu.make_async_copy(source, mid, arrived.at[index])
+        for index, (source, mid) in enumerate(zip(sources, held))
+    ]
+    second = [
+        pltpu.make_async_copy(mid, sink, left.at[index])
+        for index, (mid, sink) in enumerate(zip(held, sinks))
+    ]
+    for copy in first:
+        copy.start()
+    for before, after in zip(first, second):
+        before.wait()
+        after.start()
+    for copy in second:
+        copy.wait()
+
+
 def local(query_proj, key_proj, value_proj, out_grad, gate_scale):
-    whole = pl.BlockSpec(memory_space=pl.ANY)
+    whole = pl.BlockSpec(memory_space=pltpu.HBM)
+    some = pl.BlockSpec(memory_space=pl.ANY)
     small = pl.BlockSpec(memory_space=pltpu.VMEM)
     big = jax.ShapeDtypeStruct((1, 1, ROWS, D), jnp.bfloat16)
     unit_rows = pltpu.VMEM((TOKENS, HEAD_DIM), jnp.bfloat16)
     unit_sums = pltpu.VMEM((TOKENS, HEAD_DIM), jnp.float32)
     gate_tile = pltpu.VMEM((8, HEAD_DIM), jnp.float32)
     dma = pltpu.SemaphoreType.DMA
-    return pl.pallas_call(
+    results = pl.pallas_call(
         kernel,
         out_shape=(big, big, big, big, jax.ShapeDtypeStruct((1, D), jnp.float32)),
         in_specs=[whole] * 4 + [small],
-        out_specs=(whole, whole, whole, whole, small),
+        out_specs=(some, some, some, some, small),
         scratch_shapes=[
             unit_rows,
             unit_rows,
@@ -440,7 +476,7 @@
             dma((HEADS,)),
         ],
         compiler_params=pltpu.CompilerParams(
-            collective_id=0, has_side_effects=True, vmem_limit_bytes=50 * 2**20
+            collective_id=0, has_side_effects=True, vmem_limit_bytes=63 * 2**20
         ),
         cost_estimate=pl.CostEstimate(
             flops=12 * TOKENS * TOKENS * HEAD_DIM,
@@ -449,6 +485,14 @@
         ),
         name="heads_attention",
     )(query_proj, key_proj, value_proj, out_grad, gate_scale)
+    return pl.pallas_call(
+        hand_on,
+        out_shape=tuple(jax.ShapeDtypeStruct(r.shape, r.dtype) for r in results),
+        in_specs=[whole] * 5,
+        out_specs=(whole,) * 5,
+        scratch_shapes=[pltpu.VMEM(r.shape, r.dtype) for r in results] + [dma((5,))] * 2,
+        name="hand_on",
+    )(*results)
 
 
 def solution(mesh):

time: 104 us -> 95.4 us (0.917)
  the two profiles are of different devices: /device:TPU:48 before, /device:TPU:1 now
where the time goes in v2:
time: 95.4 us; the launch traced here: 95.1 us
  Pallas kernels  94.4 us (99%)
    pallas_call x1, Pallas kernels, local(): pl.pallas_call(kernel, out_shape=(big, big, big, big, jax.ShapeDtypeStruc...  92.2 us
    pallas_call x1, Pallas kernels, local(): pl.pallas_call(hand_on, out_shape=tuple((jax.ShapeDtypeStruct(r.shape, r....  2.22 us

profile of v2, /device:TPU:1, one launch (start us, length us, event | category | flops | bytes accessed | tf_op | source)
XLA Modules:
  0.0 95.1 jit_solution(3294027881634368365)
XLA Ops:
  0.6 92.2 %heads_attention.1 = (bf16[1,1,128,1536]{3,2,1,0:T(8,128)(2,1)}, bf16[1,1,128,1536]{3,2,1,0:T(8,128)(2,1)}, bf16[1,1,128,1536]{3,2,1,0:T(8,128)(2,1)}, bf16[1,1,128,1536]{3,2,1,0:T(8,128)(2,1)}, f32[1,1536]{1,0:T(1,128)}) custom-call(bf16[1,1,128,1536]{3,2,1,0:T(8,128)(2,1)} %query_ref.1, bf16[1,1,128,1536]{3,2,1,0:T(8,128)(2,1)} %key_ref.1, ...), custom_call_target="tpu_custom_call" | custom-call | flops 6442450944 | bytes 4194304 | tf_op jit(solution)/shard_map/heads_attention/pallas_call | solution.py:444
  92.8 2.2 %hand_on.1 = (bf16[1,1,128,1536]{3,2,1,0:T(8,128)(2,1)}, bf16[1,1,128,1536]{3,2,1,0:T(8,128)(2,1)}, bf16[1,1,128,1536]{3,2,1,0:T(8,128)(2,1)}, bf16[1,1,128,1536]{3,2,1,0:T(8,128)(2,1)}, f32[1,1536]{1,0:T(1,128)}) custom-call(bf16[1,1,128,1536]{3,2,1,0:T(8,128)(2,1)} %get-tuple-element.10.refs_0_, bf16[1,1,128,1536]{3,2,1,0:T(8,128)(2,1)} %get-tuple-element.11.refs_1_, ...), custom_call_target="tpu_custom_call" | custom-call | tf_op jit(solution)/shard_map/hand_on/pallas_call | solution.py:488

commit v3 on v2

--- a/solution.py
+++ b/solution.py
@@ -15,6 +15,7 @@
 D = HEADS * HEAD_DIM
 Z = 8
 CLIPS = 8
+UNITS = 3
 CHUNK = 256
 CHUNKS = TOKENS // CHUNK
 PER_CHUNK = CHUNK // ROWS
@@ -53,9 +54,9 @@
     dk_all,
     dv_all,
     gate_acc,
+    gate_own,
     gate_in,
-    gate_total,
-    gate_heads,
+    gate_rows,
     kv_send,
     qg_send,
     k_recv,
@@ -65,10 +66,17 @@
     rows_send,
     cols_send,
     out_recv,
+    gate_send,
+    unit_recv,
     clip_send,
     clip_recv,
-    head_send,
-    head_recv,
+    row_send,
+    row_recv,
+    final_send,
+    final_recv,
+    relay,
+    relay_recv,
+    relay_send,
 ):
     clip = lax.axis_index("dp")
     tower = lax.axis_index("tower")
@@ -80,14 +88,16 @@
     has_unit = ring % 4 != 0
     slot = (ring // 4) * 3 + lax.max(ring % 4 - 1, 0)
     head = x_hi * 6 + slot
+    idle_x = (z + 2 * core) % 4
+    idle_hi = idle_x // 2
+    unit = (2 * x_hi + tower - idle_x + 7) % 4
 
     def device(clip_to, tower_to, seq_to):
         return {"dp": clip_to, "tower": tower_to, "seq": seq_to}
 
-    def peer_clip(step):
+    def row_in(step):
         other = (clip + step) % CLIPS
-        other_z = (z + 2 * core + 16 - 2 * (other % 2)) % Z
-        return other, x_hi * Z + other_z
+        return other, (z + 2 * core + 16 - 2 * (other % 2)) % Z
 
     barrier = pltpu.get_barrier_semaphore()
 
@@ -103,15 +113,24 @@
 
     lax.fori_loop(1, 2 * BLOCKS, greet, 0)
 
-    def greet_clip(step, carry):
-        other, place = peer_clip(step)
-        pl.semaphore_signal(
-            barrier, inc=1, device_id=device(other, tower, place), device_id_type=MESH
-        )
-        return carry
-
-    lax.fori_loop(1, CLIPS, greet_clip, 0)
-    pl.semaphore_wait(barrier, 2 * BLOCKS - 1 + CLIPS - 1)
+    @pl.when(jnp.logical_not(has_unit))
+    def _():
+        def greet_clip(step, carry):
+            other, other_z = row_in(step)
+            pl.semaphore_signal(
+                barrier,
+                inc=1,
+                device_id=device(other, idle_x % 2, idle_hi * Z + other_z),
+                device_id_type=MESH,
+            )
+            return carry
+
+        lax.fori_loop(1, CLIPS, greet_clip, 0)
+        pl.semaphore_wait(barrier, 2 * BLOCKS - 1 + CLIPS - 1)
+
+    @pl.when(has_unit)
+    def _():
+        pl.semaphore_wait(barrier, 2 * BLOCKS - 1)
 
     def offset(turn):
         return ((turn + 1) // 2) * (2 * (turn % 2) - 1) * (1 - 2 * core)
@@ -202,27 +221,83 @@
             device_id_type=MESH,
         )
 
+    def passed_on(place_z):
+        return idle_hi * Z + place_z
+
+    def relay_copy(index, place_z):
+        block = passed_on(place_z)
+        return pltpu.make_async_remote_copy(
+            src_ref=(att_all, dk_all)[index].at[rows_of(block)],
+            dst_ref=relay.at[index, unit, place_z],
+            send_sem=(rows_send, cols_send)[index].at[0, block],
+            recv_sem=relay_recv.at[index, unit, place_z],
+            device_id=device(clip, idle_x % 2, passed_on(z)),
+            device_id_type=MESH,
+        )
+
+    def forward_copy(index, from_unit, place_z):
+        from_tower, from_head = unit_at(from_unit)
+        to_tower = (from_tower + index) % 2
+        return pltpu.make_async_remote_copy(
+            src_ref=relay.at[index, from_unit, place_z],
+            dst_ref=(att_ref, dk_ref)[index].at[0, 0, :, lanes_of(from_head)],
+            send_sem=relay_send.at[index, from_unit, place_z],
+            recv_sem=out_recv.at[2 * index, from_head],
+            device_id=device(clip, to_tower, passed_on(place_z)),
+            device_id_type=MESH,
+        )
+
+    gate_place = device(clip, idle_x % 2, passed_on(z))
+
+    def unit_gate_copy():
+        return pltpu.make_async_remote_copy(
+            src_ref=gate_own,
+            dst_ref=gate_in.at[clip, unit],
+            send_sem=gate_send,
+            recv_sem=unit_recv.at[unit],
+            device_id=gate_place,
+            device_id_type=MESH,
+        )
+
     def clip_copy(step):
-        other, place = peer_clip(step)
-        return pltpu.make_async_remote_copy(
-            src_ref=gate_acc,
+        other, other_z = row_in(step)
+        return pltpu.make_async_remote_copy(
+            src_ref=gate_in.at[clip],
             dst_ref=gate_in.at[clip],
             send_sem=clip_send.at[step],
             recv_sem=clip_recv.at[clip],
-            device_id=device(other, tower, place),
-            device_id_type=MESH,
-        )
-
-    def head_copy(step):
-        place = (seq + step) % BLOCKS
-        return pltpu.make_async_remote_copy(
-            src_ref=gate_total,
-            dst_ref=gate_heads.at[head],
-            send_sem=head_send.at[step],
-            recv_sem=head_recv.at[head],
-            device_id=device(clip, tower, place),
-            device_id_type=MESH,
-        )
+            device_id=device(other, idle_x % 2, idle_hi * Z + other_z),
+            device_id_type=MESH,
+        )
+
+    def row_gate_copy(step):
+        to_z = (z + step) % Z
+        to_x = (to_z + 2 * core) % 4
+        return pltpu.make_async_remote_copy(
+            src_ref=gate_rows.at[z],
+            dst_ref=gate_rows.at[z],
+            send_sem=row_send.at[step],
+            recv_sem=row_recv.at[z],
+            device_id=device(clip, to_x % 2, (to_x // 2) * Z + to_z),
+            device_id_type=MESH,
+        )
+
+    def final_gate_copy(to_unit):
+        to_x = (idle_x + 1 + to_unit) % 4
+        return pltpu.make_async_remote_copy(
+            src_ref=gate_rows,
+            dst_ref=gate_rows,
+            send_sem=final_send.at[to_unit],
+            recv_sem=final_recv,
+            device_id=device(clip, to_x % 2, (to_x // 2) * Z + z),
+            device_id_type=MESH,
+        )
+
+    def unit_at(from_unit):
+        from_x = (idle_x + 1 + from_unit) % 4
+        from_ring = (z + 2 * core + 16 - from_x) % Z
+        from_head = (from_x // 2) * 6 + (from_ring // 4) * 3 + lax.max(from_ring % 4 - 1, 0)
+        return from_x % 2, from_head
 
     @pl.when(has_unit)
     def _():
@@ -283,12 +358,20 @@
             grad_scores = (probs * (grad_probs - delta) * SCALE).astype(jnp.bfloat16)
             query_grad = jnp.dot(grad_scores, keys, preferred_element_type=jnp.float32)
             put(dq_all, query_grad.astype(jnp.bfloat16))
-            for block in blocks:
+            for part, block in enumerate(blocks):
+                passed = jnp.logical_and(part == idle_hi, chunk != z)
+
+                @pl.when(passed)
+                def _():
+                    relay_copy(0, chunk).start()
+
+                @pl.when(jnp.logical_and(block != seq, jnp.logical_not(passed)))
+                def _():
+                    row_copy(0, block).start()
 
                 @pl.when(block != seq)
                 def _():
-                    for index in range(2):
-                        row_copy(index, block).start()
+                    row_copy(1, block).start()
 
                 @pl.when(block == seq)
                 def _():
@@ -309,7 +392,56 @@
 
         lax.fori_loop(0, CHUNKS, one_chunk, 0)
 
-        gate_in[pl.ds(clip, 1)] = gate_acc[...][None]
+        gate_own[...] = jnp.sum(gate_acc[...], axis=0, keepdims=True)
+
+        unit_gate_copy().start()
+
+        dk_all[...] = dk_acc[...].astype(jnp.bfloat16)
+        dv_all[...] = dv_acc[...].astype(jnp.bfloat16)
+
+        def send_relay(step, carry):
+            relay_copy(1, (z + offset_out(step) + Z) % Z).start()
+            return carry
+
+        lax.fori_loop(0, Z - 1, send_relay, 0)
+
+        def send_columns(index):
+            def send_column(step, carry):
+                place_z = (z + offset_out(step // 2) + Z) % Z
+                place_x = (x_hi + step) % 2
+                passed = jnp.logical_and(place_x == idle_hi, place_z != z)
+
+                @pl.when(jnp.logical_or(index == 1, jnp.logical_not(passed)))
+                def _():
+                    column_copy(index, place_x * Z + place_z).start()
+
+                return carry
+
+            lax.fori_loop(0, BLOCKS, send_column, 0)
+
+        send_columns(0)
+
+        send_columns(1)
+
+    @pl.when(jnp.logical_not(has_unit))
+    def _():
+        def forward(index, place_z):
+            for from_unit in range(UNITS):
+                held = relay.at[index, from_unit, place_z]
+                pltpu.make_async_copy(
+                    held, held, relay_recv.at[index, from_unit, place_z]
+                ).wait()
+                forward_copy(index, from_unit, place_z).start()
+
+        def forward_rows(step, carry):
+            forward(0, (z - offset(step) + Z) % Z)
+            return carry
+
+        lax.fori_loop(1, CHUNKS, forward_rows, 0)
+
+        for from_unit in range(UNITS):
+            there = gate_in.at[clip, from_unit]
+            pltpu.make_async_copy(there, there, unit_recv.at[from_unit]).wait()
 
         def send_clip(step, carry):
             clip_copy(step).start()
@@ -317,53 +449,52 @@
 
         lax.fori_loop(1, CLIPS, send_clip, 0)
 
-        dk_all[...] = dk_acc[...].astype(jnp.bfloat16)
-        dv_all[...] = dv_acc[...].astype(jnp.bfloat16)
-
-        def send_columns(index):
-            def send_column(step, carry):
-                block = ((x_hi + step) % 2) * Z + (z + offset_out(step // 2) + Z) % Z
-                column_copy(index, block).start()
-                return carry
-
-            lax.fori_loop(0, BLOCKS, send_column, 0)
-
-        send_columns(0)
+        def forward_columns(step, carry):
+            forward(1, (z + offset_out(step) + Z) % Z)
+            return carry
 
         def wait_clip(step, carry):
-            other = (clip + step) % CLIPS
-            pltpu.make_async_copy(gate_in.at[other], gate_in.at[other], clip_recv.at[other]).wait()
+            there = gate_in.at[(clip + step) % CLIPS]
+            pltpu.make_async_copy(there, there, clip_recv.at[(clip + step) % CLIPS]).wait()
             return carry
 
         lax.fori_loop(1, CLIPS, wait_clip, 0)
-        total = jnp.sum(jnp.sum(gate_in[...], axis=0), axis=0, keepdims=True)
-        total = jnp.broadcast_to(total, (8, HEAD_DIM))
-        gate_total[...] = total
-        gate_heads[pl.ds(head, 1)] = total[None]
-
-        def send_head(step, carry):
-            head_copy(step).start()
-            return carry
-
-        lax.fori_loop(1, BLOCKS, send_head, 0)
-        send_columns(1)
+        gate_rows[z] = jnp.sum(gate_in[...], axis=0)
+
+        def send_row(step, carry):
+            row_gate_copy(step).start()
+            return carry
+
+        lax.fori_loop(1, Z, send_row, 0)
+        lax.fori_loop(0, Z - 1, forward_columns, 0)
+
+        def wait_row(step, carry):
+            there = gate_rows.at[(z + step) % Z]
+            pltpu.make_async_copy(there, there, row_recv.at[(z + step) % Z]).wait()
+            return carry
+
+        lax.fori_loop(1, Z, wait_row, 0)
+        for to_unit in range(UNITS):
+            final_gate_copy(to_unit).start()
 
     def wait_outputs(from_head, carry):
         for index, sink in enumerate((att_ref, dq_ref, dk_ref, dv_ref)):
             there = sink.at[0, 0, :, lanes_of(from_head)]
             pltpu.make_async_copy(there, there, out_recv.at[index, from_head]).wait()
 
-        @pl.when(jnp.logical_or(from_head != head, jnp.logical_not(has_unit)))
-        def _():
-            there = gate_heads.at[from_head]
-            pltpu.make_async_copy(there, there, head_recv.at[from_head]).wait()
-
         return carry
 
     lax.fori_loop(0, HEADS, wait_outputs, 0)
+
+    @pl.when(has_unit)
+    def _():
+        pltpu.make_async_copy(gate_rows, gate_rows, final_recv).wait()
+
     for from_head in range(HEADS):
-        gate_grad_ref[:, from_head * HEAD_DIM : (from_head + 1) * HEAD_DIM] = gate_heads[
-            from_head, 0:1
+        from_ring = from_head % 6 // 3 * 4 + from_head % 3 + 1
+        from_z = (from_ring + 2 * (from_head // 6) + tower + 16 - 2 * core) % Z
+        gate_grad_ref[:, from_head * HEAD_DIM : (from_head + 1) * HEAD_DIM] = gate_rows[
+            from_z, 3 - from_ring % 4
         ]
 
     def wait_inputs_sent(step, carry):
@@ -400,17 +531,27 @@
 
         lax.fori_loop(0, BLOCKS, wait_sent, 0)
 
-        def wait_clip_sent(step, carry):
+        unit_gate_copy().wait_send()
+
+    @pl.when(jnp.logical_not(has_unit))
+    def _():
+        def wait_forwarded(step, carry):
+            place_z = (z + step) % Z
+            for index in range(2):
+                for from_unit in range(UNITS):
+                    forward_copy(index, from_unit, place_z).wait_send()
+            return carry
+
+        lax.fori_loop(1, Z, wait_forwarded, 0)
+
+        def wait_gate_sent(step, carry):
             clip_copy(step).wait_send()
-            return carry
-
-        lax.fori_loop(1, CLIPS, wait_clip_sent, 0)
-
-        def wait_head_sent(step, carry):
-            head_copy(step).wait_send()
-            return carry
-
-        lax.fori_loop(1, BLOCKS, wait_head_sent, 0)
+            row_gate_copy(step).wait_send()
+            return carry
+
+        lax.fori_loop(1, Z, wait_gate_sent, 0)
+        for to_unit in range(UNITS):
+            final_gate_copy(to_unit).wait_send()
 
 
 def hand_on(*refs):
@@ -439,7 +580,6 @@
     big = jax.ShapeDtypeStruct((1, 1, ROWS, D), jnp.bfloat16)
     unit_rows = pltpu.VMEM((TOKENS, HEAD_DIM), jnp.bfloat16)
     unit_sums = pltpu.VMEM((TOKENS, HEAD_DIM), jnp.float32)
-    gate_tile = pltpu.VMEM((8, HEAD_DIM), jnp.float32)
     dma = pltpu.SemaphoreType.DMA
     results = pl.pallas_call(
         kernel,
@@ -457,10 +597,10 @@
             unit_sums,
             unit_rows,
             unit_rows,
-            gate_tile,
-            pltpu.VMEM((CLIPS, 8, HEAD_DIM), jnp.float32),
-            gate_tile,
-            pltpu.VMEM((HEADS, 8, HEAD_DIM), jnp.float32),
+            pltpu.VMEM((8, HEAD_DIM), jnp.float32),
+            pltpu.VMEM((1, HEAD_DIM), jnp.float32),
+            pltpu.VMEM((CLIPS, UNITS, 1, HEAD_DIM), jnp.float32),
+            pltpu.VMEM((Z, UNITS, 1, HEAD_DIM), jnp.float32),
             dma((2, HEADS)),
             dma((2, HEADS)),
             dma((BLOCKS,)),
@@ -470,10 +610,17 @@
             dma((2, BLOCKS)),
             dma((2, BLOCKS)),
             dma((4, HEADS)),
+            dma,
+            dma((UNITS,)),
             dma((CLIPS,)),
             dma((CLIPS,)),
-            dma((BLOCKS,)),
-            dma((HEADS,)),
+            dma((Z,)),
+            dma((Z,)),
+            dma((UNITS,)),
+            dma,
+            pltpu.VMEM((2, UNITS, Z, ROWS, HEAD_DIM), jnp.bfloat16),
+            dma((2, UNITS, Z)),
+            dma((2, UNITS, Z)),
         ],
         compiler_params=pltpu.CompilerParams(
             collective_id=0, has_side_effects=True, vmem_limit_bytes=63 * 2**20

time: 95.4 us -> 90 us (0.943)
  Pallas kernels: 94.4 us -> 89.2 us
    pallas_call x1, Pallas kernels: 92.2 us -> 86.9 us  [local(): pl.pallas_call(kernel, out_shape=(big, big, big, big, jax.ShapeDtypeStruc...]
where the time goes in v3:
time: 90 us; the launch traced here: 89.8 us
  Pallas kernels  89.2 us (99%)
    pallas_call x1, Pallas kernels, local(): pl.pallas_call(kernel, out_shape=(big, big, big, big, jax.ShapeDtypeStruc...  86.9 us
    pallas_call x1, Pallas kernels, local(): pl.pallas_call(hand_on, out_shape=tuple((jax.ShapeDtypeStruct(r.shape, r....  2.22 us

profile of v3, /device:TPU:1, one launch (start us, length us, event | category | flops | bytes accessed | tf_op | source)
XLA Modules:
  0.0 89.8 jit_solution(5785410393653401277)
XLA Ops:
  0.6 86.9 %heads_attention.1 = (bf16[1,1,128,1536]{3,2,1,0:T(8,128)(2,1)}, bf16[1,1,128,1536]{3,2,1,0:T(8,128)(2,1)}, bf16[1,1,128,1536]{3,2,1,0:T(8,128)(2,1)}, bf16[1,1,128,1536]{3,2,1,0:T(8,128)(2,1)}, f32[1,1536]{1,0:T(1,128)}) custom-call(bf16[1,1,128,1536]{3,2,1,0:T(8,128)(2,1)} %query_ref.1, bf16[1,1,128,1536]{3,2,1,0:T(8,128)(2,1)} %key_ref.1, ...), custom_call_target="tpu_custom_call" | custom-call | flops 6442450944 | bytes 4194304 | tf_op jit(solution)/shard_map/heads_attention/pallas_call | solution.py:584
  87.6 2.2 %hand_on.1 = (bf16[1,1,128,1536]{3,2,1,0:T(8,128)(2,1)}, bf16[1,1,128,1536]{3,2,1,0:T(8,128)(2,1)}, bf16[1,1,128,1536]{3,2,1,0:T(8,128)(2,1)}, bf16[1,1,128,1536]{3,2,1,0:T(8,128)(2,1)}, f32[1,1536]{1,0:T(1,128)}) custom-call(bf16[1,1,128,1536]{3,2,1,0:T(8,128)(2,1)} %get-tuple-element.10.refs_0_, bf16[1,1,128,1536]{3,2,1,0:T(8,128)(2,1)} %get-tuple-element.11.refs_1_, ...), custom_call_target="tpu_custom_call" | custom-call | tf_op jit(solution)/shard_map/hand_on/pallas_call | solution.py:635

commit v4 on v3

--- a/solution.py
+++ b/solution.py
@@ -43,6 +43,9 @@
     dk_ref,
     dv_ref,
     gate_grad_ref,
+    gate_row_in,
+    gate_row_out,
+    gate_moved,
     q_all,
     k_all,
     v_all,
@@ -111,7 +114,7 @@
         )
         return carry
 
-    lax.fori_loop(1, 2 * BLOCKS, greet, 0)
+    lax.fori_loop(1, 2 * BLOCKS, greet, 0, unroll=True)
 
     @pl.when(jnp.logical_not(has_unit))
     def _():
@@ -132,6 +135,9 @@
     def _():
         pl.semaphore_wait(barrier, 2 * BLOCKS - 1)
 
+    gate_here = pltpu.make_async_copy(gate_ref, gate_row_in, gate_moved.at[0])
+    gate_here.start()
+
     def offset(turn):
         return ((turn + 1) // 2) * (2 * (turn % 2) - 1) * (1 - 2 * core)
 
@@ -139,15 +145,15 @@
         turn = 7 - turn
         return ((turn + 1) // 2) * (2 * (turn % 2) - 1) * (1 - 2 * core)
 
-    def target(step, tower_to):
+    def target(step, tower_to, far=False):
         to_x = (x_hi + step) % 2
-        to_z = (z + offset(step // 2) + Z) % Z
+        to_z = (z + offset(7 - step // 2 if far else step // 2) + Z) % Z
         to_ring = (to_z + 2 * core + 16 - 2 * to_x - tower_to) % Z
         to_head = to_x * 6 + (to_ring // 4) * 3 + lax.max(to_ring % 4 - 1, 0)
         return to_ring % 4 != 0, to_head, to_x * Z + to_z
 
     def send_kv(step, carry):
-        there, to_head, place = target(step, 1 - tower)
+        there, to_head, place = target(step, 1 - tower, True)
 
         @pl.when(there)
         def _():
@@ -299,9 +305,11 @@
         from_head = (from_x // 2) * 6 + (from_ring // 4) * 3 + lax.max(from_ring % 4 - 1, 0)
         return from_x % 2, from_head
 
+    gate_here.wait()
+
     @pl.when(has_unit)
     def _():
-        gate_row = gate_ref[:, lanes_of(head)]
+        gate_row = gate_row_in[:, lanes_of(head)]
         gate_acc[...] = jnp.zeros_like(gate_acc)
         dk_acc[...] = jnp.zeros_like(dk_acc)
         dv_acc[...] = jnp.zeros_like(dv_acc)
@@ -477,6 +485,19 @@
         for to_unit in range(UNITS):
             final_gate_copy(to_unit).start()
 
+    @pl.when(has_unit)
+    def _():
+        pltpu.make_async_copy(gate_rows, gate_rows, final_recv).wait()
+
+    for from_head in range(HEADS):
+        from_ring = from_head % 6 // 3 * 4 + from_head % 3 + 1
+        from_z = (from_ring + 2 * (from_head // 6) + tower + 16 - 2 * core) % Z
+        gate_row_out[:, from_head * HEAD_DIM : (from_head + 1) * HEAD_DIM] = gate_rows[
+            from_z, 3 - from_ring % 4
+        ]
+    gate_gone = pltpu.make_async_copy(gate_row_out, gate_grad_ref, gate_moved.at[1])
+    gate_gone.start()
+
     def wait_outputs(from_head, carry):
         for index, sink in enumerate((att_ref, dq_ref, dk_ref, dv_ref)):
             there = sink.at[0, 0, :, lanes_of(from_head)]
@@ -486,19 +507,8 @@
 
     lax.fori_loop(0, HEADS, wait_outputs, 0)
 
-    @pl.when(has_unit)
-    def _():
-        pltpu.make_async_copy(gate_rows, gate_rows, final_recv).wait()
-
-    for from_head in range(HEADS):
-        from_ring = from_head % 6 // 3 * 4 + from_head % 3 + 1
-        from_z = (from_ring + 2 * (from_head // 6) + tower + 16 - 2 * core) % Z
-        gate_grad_ref[:, from_head * HEAD_DIM : (from_head + 1) * HEAD_DIM] = gate_rows[
-            from_z, 3 - from_ring % 4
-        ]
-
     def wait_inputs_sent(step, carry):
-        there, to_head, place = target(step, 1 - tower)
+        there, to_head, place = target(step, 1 - tower, True)
 
         @pl.when(there)
         def _():
@@ -552,6 +562,8 @@
         lax.fori_loop(1, Z, wait_gate_sent, 0)
         for to_unit in range(UNITS):
             final_gate_copy(to_unit).wait_send()
+
+    gate_gone.wait()
 
 
 def hand_on(*refs):
@@ -574,9 +586,7 @@
 
 
 def local(query_proj, key_proj, value_proj, out_grad, gate_scale):
-    whole = pl.BlockSpec(memory_space=pltpu.HBM)
-    some = pl.BlockSpec(memory_space=pl.ANY)
-    small = pl.BlockSpec(memory_space=pltpu.VMEM)
+    whole = pl.BlockSpec(memory_space=pl.ANY)
     big = jax.ShapeDtypeStruct((1, 1, ROWS, D), jnp.bfloat16)
     unit_rows = pltpu.VMEM((TOKENS, HEAD_DIM), jnp.bfloat16)
     unit_sums = pltpu.VMEM((TOKENS, HEAD_DIM), jnp.float32)
@@ -584,9 +594,12 @@
     results = pl.pallas_call(
         kernel,
         out_shape=(big, big, big, big, jax.ShapeDtypeStruct((1, D), jnp.float32)),
-        in_specs=[whole] * 4 + [small],
-        out_specs=(some, some, some, some, small),
+        in_specs=[whole] * 5,
+        out_specs=(whole,) * 5,
         scratch_shapes=[
+            pltpu.VMEM((1, D), jnp.float32),
+            pltpu.VMEM((1, D), jnp.float32),
+            dma((2,)),
             unit_rows,
             unit_rows,
             unit_rows,

time: 90 us -> 88.4 us (0.982)
  Pallas kernels: 89.2 us -> 87.7 us
    pallas_call x1, Pallas kernels: 86.9 us -> 85.5 us  [local(): pl.pallas_call(kernel, out_shape=(big, big, big, big, jax.ShapeDtypeStruc...]
where the time goes in v4:
time: 88.4 us; the launch traced here: 88.3 us
  Pallas kernels  87.7 us (99%)
    pallas_call x1, Pallas kernels, local(): pl.pallas_call(kernel, out_shape=(big, big, big, big, jax.ShapeDtypeStruc...  85.5 us
    pallas_call x1, Pallas kernels, local(): pl.pallas_call(hand_on, out_shape=tuple((jax.ShapeDtypeStruct(r.shape, r....  2.22 us

profile of v4, /device:TPU:1, one launch (start us, length us, event | category | flops | bytes accessed | tf_op | source)
XLA Modules:
  0.0 88.3 jit_solution(6505426450050457782)
XLA Ops:
  0.6 85.5 %heads_attention.1 = (bf16[1,1,128,1536]{3,2,1,0:T(8,128)(2,1)}, bf16[1,1,128,1536]{3,2,1,0:T(8,128)(2,1)}, bf16[1,1,128,1536]{3,2,1,0:T(8,128)(2,1)}, bf16[1,1,128,1536]{3,2,1,0:T(8,128)(2,1)}, f32[1,1536]{1,0:T(1,128)}) custom-call(bf16[1,1,128,1536]{3,2,1,0:T(8,128)(2,1)} %query_ref.1, bf16[1,1,128,1536]{3,2,1,0:T(8,128)(2,1)} %key_ref.1, ...), custom_call_target="tpu_custom_call" | custom-call | flops 6442450944 | bytes 4194304 | tf_op jit(solution)/shard_map/heads_attention/pallas_call | solution.py:594
  86.1 2.2 %hand_on.1 = (bf16[1,1,128,1536]{3,2,1,0:T(8,128)(2,1)}, bf16[1,1,128,1536]{3,2,1,0:T(8,128)(2,1)}, bf16[1,1,128,1536]{3,2,1,0:T(8,128)(2,1)}, bf16[1,1,128,1536]{3,2,1,0:T(8,128)(2,1)}, f32[1,1536]{1,0:T(1,128)}) custom-call(bf16[1,1,128,1536]{3,2,1,0:T(8,128)(2,1)} %get-tuple-element.10.refs_0_, bf16[1,1,128,1536]{3,2,1,0:T(8,128)(2,1)} %get-tuple-element.11.refs_1_, ...), custom_call_target="tpu_custom_call" | custom-call | tf_op jit(solution)/shard_map/hand_on/pallas_call | solution.py:648

commit v5 on v4

--- a/solution.py
+++ b/solution.py
@@ -22,6 +22,10 @@
 SCALE = 1.0 / math.sqrt(HEAD_DIM)
 EXP2_SCALE = SCALE * math.log2(math.e)
 MESH = pl.DeviceIdType.MESH
+
+
+def wait_for(ref, done):
+    pltpu.make_async_copy(ref, ref, done).wait()
 
 
 def rows_of(block):
@@ -163,8 +167,8 @@
                 pltpu.make_async_remote_copy(
                     src_ref=source.at[0, 0, :, lanes_of(to_head)],
                     dst_ref=sink.at[rows_of(seq)],
-                    send_sem=kv_send.at[index, to_head],
-                    recv_sem=arrived.at[seq],
+                    send_sem=kv_send.at[index],
+                    recv_sem=arrived,
                     device_id=device(clip, 1 - tower, place),
                     device_id_type=MESH,
                 ).start()
@@ -178,7 +182,7 @@
         return pltpu.make_async_remote_copy(
             src_ref=source.at[0, 0, :, lanes_of(to_head)],
             dst_ref=sink.at[rows_of(seq)],
-            send_sem=qg_send.at[index, to_head],
+            send_sem=qg_send.at[index],
             recv_sem=arrived.at[seq],
             device_id=device(clip, tower, place),
             device_id_type=MESH,
@@ -210,8 +214,8 @@
         return pltpu.make_async_remote_copy(
             src_ref=source.at[rows_of(block)],
             dst_ref=sink.at[0, 0, :, lanes_of(head)],
-            send_sem=rows_send.at[index, block],
-            recv_sem=out_recv.at[index, head],
+            send_sem=rows_send.at[index],
+            recv_sem=out_recv.at[index],
             device_id=device(clip, tower, block),
             device_id_type=MESH,
         )
@@ -221,8 +225,8 @@
         return pltpu.make_async_remote_copy(
             src_ref=source.at[rows_of(block)],
             dst_ref=sink.at[0, 0, :, lanes_of(head)],
-            send_sem=cols_send.at[index, block],
-            recv_sem=out_recv.at[2 + index, head],
+            send_sem=cols_send.at[index],
+            recv_sem=out_recv.at[2 + index],
             device_id=device(clip, 1 - tower, block),
             device_id_type=MESH,
         )
@@ -235,7 +239,7 @@
         return pltpu.make_async_remote_copy(
             src_ref=(att_all, dk_all)[index].at[rows_of(block)],
             dst_ref=relay.at[index, unit, place_z],
-            send_sem=(rows_send, cols_send)[index].at[0, block],
+            send_sem=(rows_send, cols_send)[index].at[0],
             recv_sem=relay_recv.at[index, unit, place_z],
             device_id=device(clip, idle_x % 2, passed_on(z)),
             device_id_type=MESH,
@@ -247,8 +251,8 @@
         return pltpu.make_async_remote_copy(
             src_ref=relay.at[index, from_unit, place_z],
             dst_ref=(att_ref, dk_ref)[index].at[0, 0, :, lanes_of(from_head)],
-            send_sem=relay_send.at[index, from_unit, place_z],
-            recv_sem=out_recv.at[2 * index, from_head],
+            send_sem=relay_send,
+            recv_sem=out_recv.at[2 * index],
             device_id=device(clip, to_tower, passed_on(place_z)),
             device_id_type=MESH,
         )
@@ -270,8 +274,8 @@
         return pltpu.make_async_remote_copy(
             src_ref=gate_in.at[clip],
             dst_ref=gate_in.at[clip],
-            send_sem=clip_send.at[step],
-            recv_sem=clip_recv.at[clip],
+            send_sem=clip_send,
+            recv_sem=clip_recv,
             device_id=device(other, idle_x % 2, idle_hi * Z + other_z),
             device_id_type=MESH,
         )
@@ -282,8 +286,8 @@
         return pltpu.make_async_remote_copy(
             src_ref=gate_rows.at[z],
             dst_ref=gate_rows.at[z],
-            send_sem=row_send.at[step],
-            recv_sem=row_recv.at[z],
+            send_sem=row_send,
+            recv_sem=row_recv,
             device_id=device(clip, to_x % 2, (to_x // 2) * Z + to_z),
             device_id_type=MESH,
         )
@@ -314,16 +318,8 @@
         dk_acc[...] = jnp.zeros_like(dk_acc)
         dv_acc[...] = jnp.zeros_like(dv_acc)
 
-        def wait_kv(block, carry):
-            pltpu.make_async_copy(
-                k_all.at[rows_of(block)], k_all.at[rows_of(block)], k_recv.at[block]
-            ).wait()
-            pltpu.make_async_copy(
-                v_all.at[rows_of(block)], v_all.at[rows_of(block)], v_recv.at[block]
-            ).wait()
-            return carry
-
-        lax.fori_loop(0, BLOCKS, wait_kv, 0)
+        wait_for(k_all, k_recv)
+        wait_for(v_all, v_recv)
 
         def one_chunk(step, carry):
             chunk = (z - offset(step) + Z) % Z
@@ -387,7 +383,7 @@
                         pltpu.make_async_copy(
                             source.at[rows_of(block)],
                             sink.at[0, 0, :, lanes_of(head)],
-                            out_recv.at[index, head],
+                            out_recv.at[index],
                         ).start()
 
             dk_acc[...] += lax.dot_general(
@@ -461,12 +457,7 @@
             forward(1, (z + offset_out(step) + Z) % Z)
             return carry
 
-        def wait_clip(step, carry):
-            there = gate_in.at[(clip + step) % CLIPS]
-            pltpu.make_async_copy(there, there, clip_recv.at[(clip + step) % CLIPS]).wait()
-            return carry
-
-        lax.fori_loop(1, CLIPS, wait_clip, 0)
+        wait_for(gate_in.at[pl.ds(0, CLIPS - 1)], clip_recv)
         gate_rows[z] = jnp.sum(gate_in[...], axis=0)
 
         def send_row(step, carry):
@@ -476,18 +467,33 @@
         lax.fori_loop(1, Z, send_row, 0)
         lax.fori_loop(0, Z - 1, forward_columns, 0)
 
-        def wait_row(step, carry):
-            there = gate_rows.at[(z + step) % Z]
-            pltpu.make_async_copy(there, there, row_recv.at[(z + step) % Z]).wait()
-            return carry
-
-        lax.fori_loop(1, Z, wait_row, 0)
+        wait_for(gate_rows.at[pl.ds(0, Z - 1)], row_recv)
         for to_unit in range(UNITS):
             final_gate_copy(to_unit).start()
 
+    wait_for(key_ref, kv_send.at[0])
+    wait_for(value_ref, kv_send.at[1])
+
     @pl.when(has_unit)
     def _():
-        pltpu.make_async_copy(gate_rows, gate_rows, final_recv).wait()
+        others = pl.ds(0, TOKENS - ROWS)
+        rest = pl.ds(0, D - HEAD_DIM)
+        for index in range(2):
+            wait_for(query_ref.at[0, 0, :, rest], qg_send.at[index])
+            wait_for(att_all.at[others], rows_send.at[index])
+            wait_for(dk_all, cols_send.at[index])
+        unit_gate_copy().wait_send()
+        wait_for(gate_rows, final_recv)
+
+    @pl.when(jnp.logical_not(has_unit))
+    def _():
+        for index in range(2):
+            wait_for(query_ref, qg_send.at[index])
+        wait_for(relay.at[:, :, pl.ds(0, Z - 1)], relay_send)
+        wait_for(gate_in.at[pl.ds(0, CLIPS - 1)], clip_send)
+        wait_for(gate_rows.at[pl.ds(0, Z - 1)], row_send)
+        for to_unit in range(UNITS):
+            final_gate_copy(to_unit).wait_send()
 
     for from_head in range(HEADS):
         from_ring = from_head % 6 // 3 * 4 + from_head % 3 + 1
@@ -497,72 +503,8 @@
         ]
     gate_gone = pltpu.make_async_copy(gate_row_out, gate_grad_ref, gate_moved.at[1])
     gate_gone.start()
-
-    def wait_outputs(from_head, carry):
-        for index, sink in enumerate((att_ref, dq_ref, dk_ref, dv_ref)):
-            there = sink.at[0, 0, :, lanes_of(from_head)]
-            pltpu.make_async_copy(there, there, out_recv.at[index, from_head]).wait()
-
-        return carry
-
-    lax.fori_loop(0, HEADS, wait_outputs, 0)
-
-    def wait_inputs_sent(step, carry):
-        there, to_head, place = target(step, 1 - tower, True)
-
-        @pl.when(there)
-        def _():
-            for index, source in enumerate((key_ref, value_ref)):
-                part = source.at[0, 0, :, lanes_of(to_head)]
-                pltpu.make_async_copy(part, part, kv_send.at[index, to_head]).wait()
-
-        there, to_head, place = target(step, tower)
-
-        @pl.when(jnp.logical_and(there, place != seq))
-        def _():
-            for index in range(2):
-                query_copy(index, to_head, place).wait_send()
-
-        return carry
-
-    lax.fori_loop(0, BLOCKS, wait_inputs_sent, 0)
-
-    @pl.when(has_unit)
-    def _():
-        def wait_sent(block, carry):
-            for index in range(2):
-
-                @pl.when(block != seq)
-                def _():
-                    row_copy(index, block).wait_send()
-
-                column_copy(index, block).wait_send()
-            return carry
-
-        lax.fori_loop(0, BLOCKS, wait_sent, 0)
-
-        unit_gate_copy().wait_send()
-
-    @pl.when(jnp.logical_not(has_unit))
-    def _():
-        def wait_forwarded(step, carry):
-            place_z = (z + step) % Z
-            for index in range(2):
-                for from_unit in range(UNITS):
-                    forward_copy(index, from_unit, place_z).wait_send()
-            return carry
-
-        lax.fori_loop(1, Z, wait_forwarded, 0)
-
-        def wait_gate_sent(step, carry):
-            clip_copy(step).wait_send()
-            row_gate_copy(step).wait_send()
-            return carry
-
-        lax.fori_loop(1, Z, wait_gate_sent, 0)
-        for to_unit in range(UNITS):
-            final_gate_copy(to_unit).wait_send()
-
+    for index, sink in enumerate((att_ref, dq_ref, dk_ref, dv_ref)):
+        wait_for(sink, out_recv.at[index])
     gate_gone.wait()
 
 
@@ -614,26 +556,26 @@
             pltpu.VMEM((1, HEAD_DIM), jnp.float32),
             pltpu.VMEM((CLIPS, UNITS, 1, HEAD_DIM), jnp.float32),
             pltpu.VMEM((Z, UNITS, 1, HEAD_DIM), jnp.float32),
-            dma((2, HEADS)),
-            dma((2, HEADS)),
+            dma((2,)),
+            dma((2,)),
+            dma,
+            dma,
             dma((BLOCKS,)),
             dma((BLOCKS,)),
-            dma((BLOCKS,)),
-            dma((BLOCKS,)),
-            dma((2, BLOCKS)),
-            dma((2, BLOCKS)),
-            dma((4, HEADS)),
+            dma((2,)),
+            dma((2,)),
+            dma((4,)),
             dma,
             dma((UNITS,)),
-            dma((CLIPS,)),
-            dma((CLIPS,)),
-            dma((Z,)),
-            dma((Z,)),
+            dma,
+            dma,
+            dma,
+            dma,
             dma((UNITS,)),
             dma,
             pltpu.VMEM((2, UNITS, Z, ROWS, HEAD_DIM), jnp.bfloat16),
             dma((2, UNITS, Z)),
-            dma((2, UNITS, Z)),
+            dma,
         ],
         compiler_params=pltpu.CompilerParams(
             collective_id=0, has_side_effects=True, vmem_limit_bytes=63 * 2**20

time: 88.4 us -> 84.9 us (0.960)
  Pallas kernels: 87.7 us -> 84.2 us
    pallas_call x1, Pallas kernels: 85.5 us -> 82 us  [local(): pl.pallas_call(kernel, out_shape=(big, big, big, big, jax.ShapeDtypeStruc...]
where the time goes in v5:
time: 84.9 us; the launch traced here: 84.8 us
  Pallas kernels  84.2 us (99%)
    pallas_call x1, Pallas kernels, local(): pl.pallas_call(kernel, out_shape=(big, big, big, big, jax.ShapeDtypeStruc...  82 us
    pallas_call x1, Pallas kernels, local(): pl.pallas_call(hand_on, out_shape=tuple((jax.ShapeDtypeStruct(r.shape, r....  2.22 us

profile of v5, /device:TPU:1, one launch (start us, length us, event | category | flops | bytes accessed | tf_op | source)
XLA Modules:
  0.0 84.8 jit_solution(10119895265540747567)
XLA Ops:
  0.6 82.0 %heads_attention.1 = (bf16[1,1,128,1536]{3,2,1,0:T(8,128)(2,1)}, bf16[1,1,128,1536]{3,2,1,0:T(8,128)(2,1)}, bf16[1,1,128,1536]{3,2,1,0:T(8,128)(2,1)}, bf16[1,1,128,1536]{3,2,1,0:T(8,128)(2,1)}, f32[1,1536]{1,0:T(1,128)}) custom-call(bf16[1,1,128,1536]{3,2,1,0:T(8,128)(2,1)} %query_ref.1, bf16[1,1,128,1536]{3,2,1,0:T(8,128)(2,1)} %key_ref.1, ...), custom_call_target="tpu_custom_call" | custom-call | flops 6442450944 | bytes 4194304 | tf_op jit(solution)/shard_map/heads_attention/pallas_call | solution.py:536
  82.6 2.2 %hand_on.1 = (bf16[1,1,128,1536]{3,2,1,0:T(8,128)(2,1)}, bf16[1,1,128,1536]{3,2,1,0:T(8,128)(2,1)}, bf16[1,1,128,1536]{3,2,1,0:T(8,128)(2,1)}, bf16[1,1,128,1536]{3,2,1,0:T(8,128)(2,1)}, f32[1,1536]{1,0:T(1,128)}) custom-call(bf16[1,1,128,1536]{3,2,1,0:T(8,128)(2,1)} %get-tuple-element.10.refs_0_, bf16[1,1,128,1536]{3,2,1,0:T(8,128)(2,1)} %get-tuple-element.11.refs_1_, ...), custom_call_target="tpu_custom_call" | custom-call | tf_op jit(solution)/shard_map/hand_on/pallas_call | solution.py:590

commit v6 on v5

--- a/solution.py
+++ b/solution.py
@@ -359,9 +359,9 @@
             grad_probs = lax.dot_general(
                 grad_heads, values, (((1,), (1,)), ((), ())), preferred_element_type=jnp.float32
             )
-            grad_scores = (probs * (grad_probs - delta) * SCALE).astype(jnp.bfloat16)
+            grad_scores = (probs * (grad_probs - delta)).astype(jnp.bfloat16)
             query_grad = jnp.dot(grad_scores, keys, preferred_element_type=jnp.float32)
-            put(dq_all, query_grad.astype(jnp.bfloat16))
+            put(dq_all, (query_grad * SCALE).astype(jnp.bfloat16))
             for part, block in enumerate(blocks):
                 passed = jnp.logical_and(part == idle_hi, chunk != z)
 
@@ -400,8 +400,7 @@
 
         unit_gate_copy().start()
 
-        dk_all[...] = dk_acc[...].astype(jnp.bfloat16)
-        dv_all[...] = dv_acc[...].astype(jnp.bfloat16)
+        dk_all[...] = (dk_acc[...] * SCALE).astype(jnp.bfloat16)
 
         def send_relay(step, carry):
             relay_copy(1, (z + offset_out(step) + Z) % Z).start()
@@ -425,6 +424,7 @@
 
         send_columns(0)
 
+        dv_all[...] = dv_acc[...].astype(jnp.bfloat16)
         send_columns(1)
 
     @pl.when(jnp.logical_not(has_unit))

time: 84.9 us -> 85 us (level)
  no operation moved by 1% of the time
where the time goes in v6:
time: 85 us; the launch traced here: 84.9 us
  Pallas kernels  84.2 us (99%)
    pallas_call x1, Pallas kernels, local(): pl.pallas_call(kernel, out_shape=(big, big, big, big, jax.ShapeDtypeStruc...  82 us
    pallas_call x1, Pallas kernels, local(): pl.pallas_call(hand_on, out_shape=tuple((jax.ShapeDtypeStruct(r.shape, r....  2.22 us

profile of v6, /device:TPU:1, one launch (start us, length us, event | category | flops | bytes accessed | tf_op | source)
XLA Modules:
  0.0 84.9 jit_solution(11425038910881221240)
XLA Ops:
  0.6 82.0 %heads_attention.1 = (bf16[1,1,128,1536]{3,2,1,0:T(8,128)(2,1)}, bf16[1,1,128,1536]{3,2,1,0:T(8,128)(2,1)}, bf16[1,1,128,1536]{3,2,1,0:T(8,128)(2,1)}, bf16[1,1,128,1536]{3,2,1,0:T(8,128)(2,1)}, f32[1,1536]{1,0:T(1,128)}) custom-call(bf16[1,1,128,1536]{3,2,1,0:T(8,128)(2,1)} %query_ref.1, bf16[1,1,128,1536]{3,2,1,0:T(8,128)(2,1)} %key_ref.1, ...), custom_call_target="tpu_custom_call" | custom-call | flops 6442450944 | bytes 4194304 | tf_op jit(solution)/shard_map/heads_attention/pallas_call | solution.py:536
  82.6 2.2 %hand_on.1 = (bf16[1,1,128,1536]{3,2,1,0:T(8,128)(2,1)}, bf16[1,1,128,1536]{3,2,1,0:T(8,128)(2,1)}, bf16[1,1,128,1536]{3,2,1,0:T(8,128)(2,1)}, bf16[1,1,128,1536]{3,2,1,0:T(8,128)(2,1)}, f32[1,1536]{1,0:T(1,128)}) custom-call(bf16[1,1,128,1536]{3,2,1,0:T(8,128)(2,1)} %get-tuple-element.10.refs_0_, bf16[1,1,128,1536]{3,2,1,0:T(8,128)(2,1)} %get-tuple-element.11.refs_1_, ...), custom_call_target="tpu_custom_call" | custom-call | tf_op jit(solution)/shard_map/hand_on/pallas_call | solution.py:590

commit v7 on v5

--- a/solution.py
+++ b/solution.py
@@ -235,7 +235,7 @@
         return idle_hi * Z + place_z
 
     def relay_copy(index, place_z):
-        block = passed_on(place_z)
+        block = (1 - x_hi) * Z + place_z if index == 0 else passed_on(place_z)
         return pltpu.make_async_remote_copy(
             src_ref=(att_all, dk_all)[index].at[rows_of(block)],
             dst_ref=relay.at[index, unit, place_z],
@@ -248,12 +248,14 @@
     def forward_copy(index, from_unit, place_z):
         from_tower, from_head = unit_at(from_unit)
         to_tower = (from_tower + index) % 2
+        from_hi = (idle_x + 1 + from_unit) % 4 // 2
+        to_seq = (1 - from_hi) * Z + place_z if index == 0 else passed_on(place_z)
         return pltpu.make_async_remote_copy(
             src_ref=relay.at[index, from_unit, place_z],
             dst_ref=(att_ref, dk_ref)[index].at[0, 0, :, lanes_of(from_head)],
             send_sem=relay_send,
             recv_sem=out_recv.at[2 * index],
-            device_id=device(clip, to_tower, passed_on(place_z)),
+            device_id=device(clip, to_tower, to_seq),
             device_id_type=MESH,
         )
 
@@ -363,7 +365,7 @@
             query_grad = jnp.dot(grad_scores, keys, preferred_element_type=jnp.float32)
             put(dq_all, query_grad.astype(jnp.bfloat16))
             for part, block in enumerate(blocks):
-                passed = jnp.logical_and(part == idle_hi, chunk != z)
+                passed = jnp.logical_and(part != x_hi, chunk != z)
 
                 @pl.when(passed)
                 def _():

time: 84.9 us -> 86 us (1.013)
  Pallas kernels: 84.2 us -> 85.2 us
    pallas_call x1, Pallas kernels: 82 us -> 83 us  [local(): pl.pallas_call(kernel, out_shape=(big, big, big, big, jax.ShapeDtypeStruc...]
where the time goes in v7:
time: 86 us; the launch traced here: 85.8 us
  Pallas kernels  85.2 us (99%)
    pallas_call x1, Pallas kernels, local(): pl.pallas_call(kernel, out_shape=(big, big, big, big, jax.ShapeDtypeStruc...  83 us
    pallas_call x1, Pallas kernels, local(): pl.pallas_call(hand_on, out_shape=tuple((jax.ShapeDtypeStruct(r.shape, r....  2.22 us

profile of v7, /device:TPU:1, one launch (start us, length us, event | category | flops | bytes accessed | tf_op | source)
XLA Modules:
  0.0 85.8 jit_solution(15329946476309892118)
XLA Ops:
  0.6 83.0 %heads_attention.1 = (bf16[1,1,128,1536]{3,2,1,0:T(8,128)(2,1)}, bf16[1,1,128,1536]{3,2,1,0:T(8,128)(2,1)}, bf16[1,1,128,1536]{3,2,1,0:T(8,128)(2,1)}, bf16[1,1,128,1536]{3,2,1,0:T(8,128)(2,1)}, f32[1,1536]{1,0:T(1,128)}) custom-call(bf16[1,1,128,1536]{3,2,1,0:T(8,128)(2,1)} %query_ref.1, bf16[1,1,128,1536]{3,2,1,0:T(8,128)(2,1)} %key_ref.1, ...), custom_call_target="tpu_custom_call" | custom-call | flops 6442450944 | bytes 4194304 | tf_op jit(solution)/shard_map/heads_attention/pallas_call | solution.py:538
  83.6 2.2 %hand_on.1 = (bf16[1,1,128,1536]{3,2,1,0:T(8,128)(2,1)}, bf16[1,1,128,1536]{3,2,1,0:T(8,128)(2,1)}, bf16[1,1,128,1536]{3,2,1,0:T(8,128)(2,1)}, bf16[1,1,128,1536]{3,2,1,0:T(8,128)(2,1)}, f32[1,1536]{1,0:T(1,128)}) custom-call(bf16[1,1,128,1536]{3,2,1,0:T(8,128)(2,1)} %get-tuple-element.10.refs_0_, bf16[1,1,128,1536]{3,2,1,0:T(8,128)(2,1)} %get-tuple-element.11.refs_1_, ...), custom_call_target="tpu_custom_call" | custom-call | tf_op jit(solution)/shard_map/hand_on/pallas_call | solution.py:592
